TPU v7x, 128 devices: a whole 4x4x4 slice. The times are simulated.
128 devices in a mesh: rows: 8 (over z, core), cols: 16 (over y, x).
Axes of the slice: x: 4, y: 4, z: 4, core: 2. Of those that a mesh axis runs over, the one named last changes fastest.
Arguments:
- vectors: bfloat16 [16, 524288], P(None, ('rows', 'cols')), may hold values from -6 to 6
- tree_order: int32 [524288], P(('rows', 'cols')), may hold values from 0 to 524287, as said below
- near_blocks: bfloat16 [2048, 8, 256, 256], P(('rows', 'cols')), may hold values from -0.125 to 0.125
- near_index: int32 [2048, 8], P(('rows', 'cols')), may hold values from 0 to 2047, as said below
- leaf_basis: bfloat16 [2048, 64, 256], P(('rows', 'cols')), may hold values from -0.375 to 0.375
- leaf_coupling: bfloat16 [2048, 16, 64, 64], P(('rows', 'cols')), may hold values from -0.1875 to 0.1875
- leaf_far: int32 [2048, 16], P(('rows', 'cols')), may hold values from 0 to 2047, as said below
- leaf_transfer: bfloat16 [2048, 64, 64], P(('rows', 'cols')), may hold values from -0.375 to 0.375
- node_coupling: bfloat16 [128, 8, 64, 64], P(('rows', 'cols')), may hold values from -0.25 to 0.25
- node_far: int32 [128, 8], P(('rows', 'cols')), may hold values from 0 to 127, as said below
- node_transfer: bfloat16 [128, 64, 64], P(('rows', 'cols')), may hold values from -0.375 to 0.375
- slab_coupling: bfloat16 [8, 2, 64, 64], P('rows'), may hold values from -0.5 to 0.5
- slab_far_partners: int32 [8, 2], P('rows'), may hold values from 0 to 7, as said below
Outputs:
- product: bfloat16 [16, 524288], P(None, ('rows', 'cols'))
Inputs may be any that keep to these rules, and one draw needn't show every extreme that they name: `tree_order`: a permutation that maps each aligned block of 4096 positions onto the same block of initial indices. `near_index`: the partners of a leaf are distinct leaves of its own aligned block of 256 leaves; the first is the leaf itself. `leaf_far`: distinct leaves of the leaf's own aligned block of 256 leaves, none of them among its near partners. `node_far`: distinct device-level clusters other than the cluster itself. `slab_far_partners`: distinct slab-level clusters other than the cluster itself.
All inputs are finite; a program needn't handle non-finite values.
Results may differ from a plain program's by a relative error of at most 0.00125.
Values may be sent and summed in bfloat16 or wider, within the bound.
A program may use at most 128 MiB of HBM per device.

v0:
```python
import jax
import jax.numpy as jnp
from jax import lax
from jax.sharding import PartitionSpec as P


def on_device(
    vectors,
    tree_order,
    near_blocks,
    near_index,
    leaf_basis,
    leaf_coupling,
    leaf_far,
    leaf_transfer,
    node_coupling,
    node_far,
    node_transfer,
    slab_coupling,
    slab_far_partners,
):
    highest = lax.Precision.HIGHEST
    leaf_count, rank_size, leaf_point_count = leaf_basis.shape
    rhs_count = vectors.shape[0]
    points_on_part = leaf_count * leaf_point_count
    column_count_total = lax.axis_size("cols")
    slab_size = leaf_count * column_count_total
    local_order = tree_order % points_on_part
    tree_vectors = jnp.take(vectors, local_order, axis=1)
    leaf_vectors = tree_vectors.reshape(rhs_count, leaf_count, leaf_point_count)
    leaf_coef = jnp.einsum(
        "rlb,lkb->lrk", leaf_vectors, leaf_basis, preferred_element_type=jnp.float32
    )
    near_slot = near_index % slab_size
    slab_vectors = lax.all_gather(tree_vectors, "cols", axis=1, tiled=True)
    slab_leaves = slab_vectors.reshape(rhs_count, slab_size, leaf_point_count)
    selected_entries = jnp.take(slab_leaves, near_slot, axis=1)
    near_part = jnp.einsum(
        "rlsq,lspq->rlp", selected_entries, near_blocks, preferred_element_type=jnp.float32
    )
    neighbour_coef = lax.all_gather(leaf_coef, "cols", axis=0, tiled=True)
    far_slot = leaf_far % slab_size
    leaf_out = jnp.einsum(
        "lsrm,lskm->lrk",
        neighbour_coef[far_slot],
        leaf_coupling.astype(jnp.float32),
        precision=highest,
    )
    up_leaf = leaf_transfer.astype(jnp.float32)
    node_coef = jnp.einsum("lrm,lkm->rk", leaf_coef, up_leaf, precision=highest)
    upward_node_coef = node_transfer[0].astype(jnp.float32)
    node_term = jnp.einsum("rm,km->rk", node_coef, upward_node_coef, precision=highest)
    all_nodes = lax.all_gather(node_coef[None], ("rows", "cols"), axis=0, tiled=True)
    slab_total = lax.psum(node_term, "cols")
    all_slabs = lax.all_gather(slab_total[None], "rows", axis=0, tiled=True)
    node_out = jnp.einsum(
        "srm,skm->rk",
        all_nodes[node_far[0]],
        node_coupling[0].astype(jnp.float32),
        precision=highest,
    )
    slab_out = jnp.einsum(
        "srm,skm->rk",
        all_slabs[slab_far_partners[0]],
        slab_coupling[0].astype(jnp.float32),
        precision=highest,
    )
    node_out = node_out + jnp.dot(slab_out, upward_node_coef, precision=highest)
    leaf_out = leaf_out + jnp.einsum("rk,lkm->lrm", node_out, up_leaf, precision=highest)
    far_part = jnp.einsum(
        "lrk,lkb->rlb", leaf_out, leaf_basis.astype(jnp.float32), precision=highest
    )
    tree_product = (near_part + far_part).reshape(rhs_count, points_on_part)
    product = (
        jnp.zeros((rhs_count, points_on_part), jnp.float32).at[:, local_order].set(tree_product)
    )
    return product.astype(jnp.bfloat16)


def solution(mesh):
    return jax.shard_map(
        on_device,
        mesh=mesh,
        in_specs=(
            P(None, ("rows", "cols")),
            P(("rows", "cols")),
            P(("rows", "cols"), None, None, None),
            P(("rows", "cols"), None),
            P(("rows", "cols"), None, None),
            P(("rows", "cols"), None, None, None),
            P(("rows", "cols"), None),
            P(("rows", "cols"), None, None),
            P(("rows", "cols"), None, None, None),
            P(("rows", "cols"), None),
            P(("rows", "cols"), None, None),
            P("rows", None, None, None),
            P("rows", None),
        ),
        out_specs=P(None, ("rows", "cols")),
        check_vma=False,
    )
```

profile of v0, /device:TPU:0, one launch (start us, length us, event | category | flops | bytes accessed | tf_op | source)
XLA Modules:
  0.0 232.9 jit_solution(652047431285525099)
XLA Ops:
  6.5 0.8 compare_and_fusion
  7.3 1.4 copy.37
  8.7 12.1 %gather_fusion = bf16[4096,16]{1,0:T(8,128)(2,1)S(1)} fusion(bf16[16,4096]{0,1:T(8,128)(2,1)S(1)} %copy.37, s32[4096]{0:T(1024)S(1)} %broadcast_clamp_fusion), kind=kCustom, calls=%fused_computation | custom fusion | bytes 278528 | tf_op jit(solution)/shard_map/jit(_take)/gather | solution.py:29
  20.9 0.3 copy.40
  21.2 0.9 fusion.10
  22.3 2.9 %bitcast_select_fusion = bf16[16,4096]{0,1:T(8,128)(2,1)} fusion(bf16[4096,16]{1,0:T(8,128)(2,1)S(1)} %gather_fusion, pred[4096]{0:T(1024)(128)(4,1)S(1)} %get-tuple-element.7), kind=kLoop, calls=%fused_computation.19 | loop fusion | flops 65536 | bytes 266240 | tf_op jit(solution)/shard_map/jit(_take)/select_n | solution.py:29
  25.6 0.3 convolution_bitcast_fusion.6
  26.0 64.3 %all-gather = f32[2048,64]{1,0:T(8,128)S(1)} all-gather(f32[16,64]{1,0:T(8,128)S(1)} %convolution_bitcast_fusion.6), channel_id=2, replica_groups=mesh['rows'=8,'cols'=16] {'rows','cols'}, dimensions={0}, use_global_device_ids=true | all-gather | bytes 528384 | tf_op jit(solution)/shard_map/all_gather | solution.py:53
  90.2 0.6 gather_fusion.3
  90.9 39.6 %psum.7 = f32[1,16,64]{2,1,0:T(8,128)S(1)} all-reduce(f32[1,16,64]{2,1,0:T(8,128)S(1)} %convolution_bitcast_fusion.4), channel_id=1, replica_groups=mesh['rows'=8,'cols'=16] {'cols'}, use_global_device_ids=true, to_apply=%region_0.1 | all-reduce | flops 1024 | bytes 8192 | tf_op jit(solution)/shard_map/psum | solution.py:54
  130.5 12.8 %all_gather.15 = f32[8,16,64]{2,1,0:T(8,128)S(1)} all-gather(f32[1,16,64]{2,1,0:T(8,128)S(1)} %psum.7), channel_id=1, replica_groups=mesh['rows'=8,'cols'=16] {'rows'}, dimensions={0}, use_global_device_ids=true | all-gather | bytes 36864 | tf_op jit(solution)/shard_map/all_gather | solution.py:55
  143.3 0.5 gather_fusion.4
  144.0 0.2 convolution_bitcast_fusion.5
  144.4 2.4 %gather_fusion.2 = f32[256,16,64]{2,1,0:T(8,128)S(1)} fusion(f32[256,16,64]{2,1,0:T(8,128)} %all-gather.6.cloned.1.call-done, s32[1024]{0:T(1024)S(1)} %pad_clamp_fusion.2), kind=kCustom, calls=%fused_computation.2 | custom fusion | bytes 2098176 | tf_op jit(solution)/shard_map/gather | solution.py:45
  146.8 5.2 %convolution_bitcast_fusion.1 = f32[16,16,64]{2,1,0:T(8,128)S(1)} fusion(f32[16,16,16,64]{3,2,1,0:T(8,128)S(1)} %bitcast.70, bf16[16,16,64,64]{3,2,1,0:T(8,128)(2,1)} %param.18), kind=kOutput, calls=%fused_computation.9 | convolution fusion | flops 201326592 | bytes 3211264 | tf_op jit(solution)/shard_map/lsrm,lskm->lrk/dot_general | solution.py:43
  152.0 0.2 fusion.1
  152.2 31.9 %all-gather.4.cloned.1.call-done = bf16[16,65536]{0,1:T(8,128)(2,1)} async-done(((bf16[16,4096]{0,1:T(8,128)(2,1)}), bf16[16,65536]{0,1:T(8,128)(2,1)}) %all-gather.4.cloned.1.call-update) | async-done | bytes 2097168 | tf_op jit(solution)/shard_map/all_gather | solution.py:35
  184.1 12.3 %gather_fusion.1 = bf16[128,16,256]{1,2,0:T(8,128)(2,1)} fusion(bf16[16,256,256]{0,2,1:T(8,128)(2,1)} %bitcast.75, s32[1024]{0:T(1024)S(1)} %pad_clamp_fusion.3), kind=kCustom, calls=%fused_computation.1 | custom fusion | bytes 2097664 | tf_op jit(solution)/shard_map/jit(_take)/gather | solution.py:37
  196.4 6.9 %copy.39 = bf16[128,16,256]{2,1,0:T(8,128)(2,1)S(1)} copy(bf16[128,16,256]{1,2,0:T(8,128)(2,1)} %gather_fusion.1) | data formatting | bytes 2097152 | tf_op jit(solution)/shard_map/jit(_take)/gather | solution.py:37
  203.3 8.1 %convolution_bitcast_fusion = f32[16,16,256]{2,1,0:T(8,128)S(1)} fusion(bf16[16,8,256,256]{3,2,1,0:T(8,128)(2,1)} %param.15, bf16[16,8,16,256]{3,2,1,0:T(8,128)(2,1)S(1)} %bitcast.72, pred[16,8]{1,0:T(8,128)(4,1)S(1)} %copy.36), kind=kOutput, calls=%fused_computation.8 | convolution fusion | flops 268959744 | bytes 18088064 | tf_op jit(solution)/shard_map/rlsq,lspq->rlp/dot_general | solution.py:38
  211.4 0.3 fusion
  211.7 1.9 copy.42
  213.7 11.4 %scatter_custom_fusion = f32[16,4096]{0,1:T(8,128)S(1)} fusion(s32[4096]{0:T(1024)S(1)} %get-tuple-element.8, f32[4096,16]{1,0:T(8,128)} %copy.42, f32[]{:T(128)} %constant.65.clone.1), kind=kCustom, calls=%fused_computation.21 | custom fusion | bytes 262656 | tf_op jit(solution)/shard_map/scatter | solution.py:75
  225.1 1.0 copy.43
  (43 shorter events, 1.0 us)
Async XLA Ops:
  6.5 14.7 %copy-start = (bf16[16,64,256]{2,1,0:T(8,128)(2,1)S(1)}, bf16[16,64,256]{2,1,0:T(8,128)(2,1)}, u32[]{:S(2)}) copy-start(bf16[16,64,256]{2,1,0:T(8,128)(2,1)} %param.17) | copy-start | bytes 1572868
  6.5 137.9 %all-gather.6.cloned.1.call-start = ((), (), s32[]{:S(2)}) async-start(), calls=%async_computation.1 | async-start | bytes 2228224 | tf_op jit(solution)/shard_map/all_gather | solution.py:41
  21.2 4.0 %copy-start.6 = (s32[16,16]{1,0:T(8,128)S(1)}, s32[16,16]{1,0:T(8,128)}, u32[]{:S(2)}) copy-start(s32[16,16]{1,0:T(8,128)} %param.19) | copy-start | bytes 3076
  21.2 4.1 %copy-start.7 = (s32[16,8]{0,1:T(8,128)S(1)}, s32[16,8]{0,1:T(8,128)}, u32[]{:S(2)}) copy-start(s32[16,8]{0,1:T(8,128)} %param.16) | copy-start | bytes 1540
  21.2 4.4 %copy-start.8 = (s32[1,8]{1,0:T(1,128)S(1)}, s32[1,8]{1,0:T(1,128)}, u32[]{:S(2)}) copy-start(s32[1,8]{1,0:T(1,128)} %param.22) | copy-start | bytes 100
  21.2 4.4 %copy-start.2 = (bf16[16,64,64]{2,1,0:T(8,128)(2,1)S(1)}, bf16[16,64,64]{2,1,0:T(8,128)(2,1)}, u32[]{:S(2)}) copy-start(bf16[16,64,64]{2,1,0:T(8,128)(2,1)} %param.20) | copy-start | bytes 393220
  22.2 3.5 %copy-start.1 = (f32[16,16,64]{2,1,0:T(8,128)S(1)}, f32[16,16,64]{2,1,0:T(8,128)}, u32[]{:S(2)}) copy-start(f32[16,16,64]{2,1,0:T(8,128)} %fusion.10) | copy-start | bytes 196612
  22.2 68.6 %copy-start.4 = (bf16[1,64,64]{2,1,0:T(8,128)(2,1)S(1)}, bf16[1,64,64]{2,1,0:T(8,128)(2,1)}, u32[]{:S(2)}) copy-start(bf16[1,64,64]{2,1,0:T(8,128)(2,1)} %param.23) | copy-start | bytes 24580
  22.2 121.1 %copy-start.9 = (s32[1,2]{1,0:T(1,128)S(1)}, s32[1,2]{1,0:T(1,128)}, u32[]{:S(2)}) copy-start(s32[1,2]{1,0:T(1,128)} %param.25) | copy-start | bytes 28
  22.2 121.7 %copy-start.5 = (bf16[1,2,64,64]{3,2,1,0:T(8,128)(2,1)S(1)}, bf16[1,2,64,64]{3,2,1,0:T(8,128)(2,1)}, u32[]{:S(2)}) copy-start(bf16[1,2,64,64]{3,2,1,0:T(8,128)(2,1)} %param.24) | copy-start | bytes 49156
  22.2 121.8 %copy-start.3 = (bf16[1,8,64,64]{3,2,1,0:T(8,128)(2,1)S(1)}, bf16[1,8,64,64]{3,2,1,0:T(8,128)(2,1)}, u32[]{:S(2)}) copy-start(bf16[1,8,64,64]{3,2,1,0:T(8,128)(2,1)} %param.21) | copy-start | bytes 196612
  22.2 161.9 %all-gather.4.cloned.1.call-start = ((), (), s32[]{:S(2)}) async-start(), calls=%async_computation | async-start | bytes 17825792 | tf_op jit(solution)/shard_map/all_gather | solution.py:35
Sparse Core Ops, SparseCore 0:
  22.3 47.2 all-gather.5
  71.7 112.3 all-gather.3
where the time goes:
time: 234 us; the launch traced here: 233 us
  blocking collectives  117 us (50%)
  local copies, waits for them, and re-layouts  51.3 us (22%)
  waiting for transfers between devices  31.9 us (14%)
  matrix products  15.6 us (7%)
  between operations  13.7 us (6%)
  other arithmetic  3.76 us (2%)
    all_gather x1, blocking collectives, on_device(): lax.all_gather(node_coef[None], ('rows', 'cols'), axis=0, tiled=True)  64.3 us
    psum x1, blocking collectives, on_device(): slab_total = lax.psum(node_term, 'cols')  39.6 us
    all_gather x1, waiting for transfers between devices, on_device(): slab_vectors = lax.all_gather(tree_vectors, 'cols', axis=1, tiled=True)  31.9 us
    gather x2, local copies, waits for them, and re-layouts, on_device(): selected_entries = jnp.take(slab_leaves, near_slot, axis=1)  19.2 us
    all_gather x1, blocking collectives, on_device(): all_slabs = lax.all_gather(slab_total[None], 'rows', axis=0, tiled=True)  12.8 us
    gather x2, local copies, waits for them, and re-layouts, on_device(): tree_vectors = jnp.take(vectors, local_order, axis=1)  12.4 us
    scatter x2, local copies, waits for them, and re-layouts, on_device(): jnp.zeros((rhs_count, points_on_part), jnp.float32).at[:, local_order]  12.4 us
    dot_general x1, matrix products, on_device(): jnp.einsum('rlsq,lspq->rlp', selected_entries, near_blocks, preferred_ele...  8.05 us
  transfers between devices with their start and end apart: 2, of which 1 were waited for; matrix products, arithmetic and copies ran while one was open for 6% of the time, Pallas kernels for 0%

commit v1 on v0

v1 whole, which is shorter than its diff:
```python
import jax
import jax.numpy as jnp
from jax import lax
from jax.experimental import pallas as pl
from jax.experimental.pallas import tpu as pltpu
from jax.sharding import PartitionSpec as P

MESH = pl.DeviceIdType.MESH
F32 = jnp.float32
BF16 = jnp.bfloat16

NT = (((1,), (1,)), ((), ()))
NN = (((1,), (0,)), ((), ()))


def dot(a, b, dims):
    return lax.dot_general(a, b, dims, preferred_element_type=F32)


def split2(v):
    high = v.astype(BF16)
    low = (v - high.astype(F32)).astype(BF16)
    return high, low


def dot2(v, b, dims):
    high, low = split2(v)
    rows = v.shape[0]
    both = dot(jnp.concatenate([high, low], axis=0), b, dims)
    return both[:rows] + both[rows:]


def shifted(col, dim, by):
    x, y = col % 4, col // 4
    if dim == 0:
        return y * 4 + (x + by) % 4
    return ((y + by) % 4) * 4 + x


def kernel(
    vec_hbm, ord_hbm, near_hbm, basis_hbm, coup_hbm, ltran_hbm, ncoup_hbm, ntran_hbm, scoup_hbm,
    near_idx, far_idx, node_idx, slab_idx,
    out_ref,
    vec, order, near, basis, coup, ltran, ncoup, ntran, scoup,
    onehot, wdup, x_low, x_high, coef_buf, node_buf, row_buf, near_acc, node_out_ref,
    in_sem, near_sem, send_sem, recv_sem, nsend, nrecv,
):
    col = lax.axis_index("cols")
    row = lax.axis_index("rows")
    my_x, my_y = col % 4, col // 4

    def fetch(src, dst, k):
        copy = pltpu.make_async_copy(src, dst, in_sem.at[k])
        copy.start()
        return copy

    c_vec = fetch(vec_hbm, vec, 0)
    c_ord = fetch(ord_hbm, order, 1)
    c_basis = fetch(basis_hbm, basis, 2)
    c_ltran = fetch(ltran_hbm, ltran, 3)
    c_ntran = fetch(ntran_hbm, ntran, 4)

    barrier = pltpu.get_barrier_semaphore()
    partners = [{"cols": shifted(col, dim, by)} for dim in (0, 1) for by in (1, 2, 3)]
    zrow = [(row + 2 * by) % 8 for by in (1, 2, 3)]
    other_core = row + 1 - 2 * (row % 2)
    partners += [{"rows": r} for r in zrow] + [{"rows": other_core}]
    for p in partners:
        pl.semaphore_signal(barrier, inc=1, device_id=p, device_id_type=MESH)

    c_ncoup = fetch(ncoup_hbm, ncoup, 5)
    c_scoup = fetch(scoup_hbm, scoup, 6)
    c_coup = fetch(coup_hbm, coup, 7)
    c_near = []
    for q in range(4):
        copy = pltpu.make_async_copy(
            near_hbm.at[pl.ds(4 * q, 4)], near.at[pl.ds(4 * q, 4)], near_sem.at[q]
        )
        copy.start()
        c_near.append(copy)

    c_vec.wait()
    c_ord.wait()
    lhs = jnp.concatenate([vec[:, h * 256:(h + 1) * 256] for h in range(16)], axis=0)
    level = lax.broadcasted_iota(jnp.int32, (256, 256), 0)

    def permute(leaf):
        local = order[:, leaf * 256:(leaf + 1) * 256] % 4096
        low = jnp.broadcast_to(local % 256, (256, 256))
        hot = jnp.where(low == level, 1.0, 0.0).astype(BF16)
        onehot[leaf] = hot
        part = dot(lhs, hot, NN)
        high = local // 256
        x = jnp.zeros((16, 256), F32)
        for h in range(16):
            x = x + jnp.where(high == h, part[h * 16:(h + 1) * 16], 0.0)
        return x.astype(BF16)

    own = col * 16
    slab_buf = (x_low, x_high, coef_buf)
    leaf_x = []
    for leaf in range(16):
        x = permute(leaf)
        x_low[own + leaf] = x[:, :128]
        x_high[own + leaf] = x[:, 128:]

    pl.semaphore_wait(barrier, len(partners))

    sent = []

    def chunk_copy(stage, chunk, first, count, to, k):
        span = slab_buf[stage].at[pl.ds(chunk * 16 + first, count)]
        return pltpu.make_async_remote_copy(
            span, span, send_sem.at[stage * 40 + k], recv_sem.at[stage * 40 + k],
            device_id={"cols": to}, device_id_type=MESH,
        )

    def send(stage, chunk, first, count, to, k):
        copy = chunk_copy(stage, chunk, first, count, to, k)
        copy.start()
        sent.append(copy)

    def arrived(stage, chunk, first, count, k):
        chunk_copy(stage, chunk, first, count, shifted(col, 0, 1), k).wait_recv()

    def at(half, a, b):
        return shifted(shifted(col, half, a), 1 - half, b)

    def key(half, phase, a, t):
        return half * 20 + (0 if phase == 0 else 4 + 4 * a) + t

    def dim_of(half, phase):
        return half if phase == 0 else 1 - half

    def put(stage, half, phase, a):
        d = dim_of(half, phase)
        chunk = at(half, a, 0) if phase else col
        send(stage, chunk, half * 8, 8, shifted(col, d, 1), key(half, phase, a, 0))
        send(stage, chunk, half * 8, 8, shifted(col, d, 3), key(half, phase, a, 1))

    def source(half, phase, a, by):
        return at(half, a, by) if phase else at(half, by, 0)

    def forward(stage, half, phase, a):
        d = dim_of(half, phase)
        chunk = source(half, phase, a, 3)
        arrived(stage, chunk, half * 8, 8, key(half, phase, a, 0))
        send(stage, chunk, half * 8, 4, shifted(col, d, 1), key(half, phase, a, 2))
        chunk = source(half, phase, a, 1)
        arrived(stage, chunk, half * 8, 8, key(half, phase, a, 1))
        send(stage, chunk, half * 8 + 4, 4, shifted(col, d, 3), key(half, phase, a, 3))

    def finish(stage, half, phase, a):
        chunk = source(half, phase, a, 2)
        arrived(stage, chunk, half * 8, 4, key(half, phase, a, 2))
        arrived(stage, chunk, half * 8 + 4, 4, key(half, phase, a, 3))

    def step0(stage):
        for half in (0, 1):
            put(stage, half, 0, 0)
        for half in (0, 1):
            put(stage, half, 1, 0)

    def step1(stage):
        for half in (0, 1):
            forward(stage, half, 0, 0)
        for a in (1, 3):
            for half in (0, 1):
                put(stage, half, 1, a)

    def step2(stage):
        for half in (0, 1):
            finish(stage, half, 0, 0)
        for half in (0, 1):
            put(stage, half, 1, 2)
        for half in (0, 1):
            forward(stage, half, 1, 0)

    def step3(stage, a):
        for half in (0, 1):
            forward(stage, half, 1, a)

    def step4(stage):
        for a in (0, 1, 3, 2):
            for half in (0, 1):
                finish(stage, half, 1, a)

    step0(0)

    c_basis.wait()
    c_ltran.wait()
    c_ntran.wait()
    node_coef = jnp.zeros((16, 64), F32)
    for leaf in range(16):
        coef = dot(x_low[own + leaf], basis[leaf, :, :128], NT) + dot(
            x_high[own + leaf], basis[leaf, :, 128:], NT
        )
        high, low = split2(coef)
        coef_buf[own + leaf] = jnp.concatenate([high, low], axis=1)
        node_coef = node_coef + dot2(coef, ltran[leaf], NT)
    node_term = dot2(node_coef, ntran[0], NT)

    def node_copy(src, k, to):
        return pltpu.make_async_remote_copy(
            src, src, nsend.at[k], nrecv.at[k], device_id=to, device_id_type=MESH
        )

    def node_send(src, k, to):
        copy = node_copy(src, k, to)
        copy.start()
        sent.append(copy)

    node_buf[my_y, my_x] = jnp.concatenate([node_coef, node_term], axis=1)
    for by in (1, 3, 2):
        node_send(node_buf.at[my_y, my_x], by - 1, {"cols": shifted(col, 0, by)})
    step0(1)
    step1(0)
    for by in (1, 3, 2):
        node_copy(node_buf.at[my_y, (my_x + 4 - by) % 4], by - 1, partners[0]).wait_recv()
    for by in (1, 3, 2):
        node_send(node_buf.at[my_y], 2 + by, {"cols": shifted(col, 1, by)})
    step2(0)
    for a in (1, 3, 2):
        step3(0, a)
    for by in (1, 3, 2):
        node_copy(node_buf.at[(my_y + 4 - by) % 4], 2 + by, partners[0]).wait_recv()
    slab_coef = jnp.zeros((16, 64), F32)
    for m in range(8):
        left, right = node_buf[m // 2, m % 2 * 2], node_buf[m // 2, m % 2 * 2 + 1]
        row_buf[row, m] = jnp.concatenate([left[:, :64], right[:, :64]], axis=1)
        slab_coef = slab_coef + (left[:, 64:] + right[:, 64:])
    row_buf[row, 8] = jnp.concatenate([slab_coef, slab_coef], axis=1)
    for n, by in enumerate((1, 3, 2)):
        node_send(row_buf.at[row], 6 + n, {"rows": (row + 2 * by) % 8})
    node_send(row_buf.at[row], 9, {"rows": other_core})
    step1(1)
    step4(0)
    step0(2)

    def near_part(stage, first, count):
        def body(leaf, carry):
            acc = near_acc[leaf] if stage else jnp.zeros((16, 256), F32)
            for s in range(8):
                x = slab_buf[stage][near_idx[s, leaf] % 256]
                acc = acc + dot(x, near[leaf, s, :, stage * 128:stage * 128 + 128], NT)
            near_acc[leaf] = acc
            return carry

        lax.fori_loop(first, first + count, body, 0)

    for copy in c_near:
        copy.wait()
    near_part(0, 0, 4)
    step2(1)
    step1(2)
    near_part(0, 4, 4)
    step3(1, 1)
    step3(1, 3)
    near_part(0, 8, 4)
    step3(1, 2)
    near_part(0, 12, 4)

    for n, by in enumerate((1, 3, 2)):
        node_copy(row_buf.at[(row + 8 - 2 * by) % 8], 6 + n, partners[0]).wait_recv()
        node_send(row_buf.at[(row + 8 - 2 * by) % 8], 10 + n, {"rows": other_core})
    step4(1)
    step2(2)

    c_coup.wait()

    def dup_body(leaf, carry):
        for s in range(16):
            m = coup[leaf, s]
            wdup[leaf, :, s * 128:(s + 1) * 128] = jnp.concatenate([m, m], axis=1)
        return carry

    lax.fori_loop(0, 16, dup_body, 0)

    near_part(1, 0, 4)
    step3(2, 1)
    step3(2, 3)
    near_part(1, 4, 4)
    step3(2, 2)
    near_part(1, 8, 8)

    node_copy(row_buf.at[other_core], 9, partners[0]).wait_recv()
    for n, by in enumerate((1, 3, 2)):
        node_copy(row_buf.at[(other_core + 8 - 2 * by) % 8], 10 + n, partners[0]).wait_recv()
    c_ncoup.wait()
    c_scoup.wait()
    slab_out = jnp.zeros((16, 64), F32)
    for s in range(2):
        slab_out = slab_out + dot2(row_buf[slab_idx[0, s], 8][:, :64], scoup[0, s], NT)
    node_out = dot2(slab_out, ntran[0], NN)
    lane = lax.broadcasted_iota(jnp.int32, (16, 128), 1)
    for s in range(8):
        d = node_idx[0, s]
        both = row_buf[d // 16, d % 16 // 2]
        both = jnp.where(lane // 64 == d % 2, both, 0.0)
        pair = jnp.concatenate([ncoup[0, s], ncoup[0, s]], axis=1)
        node_out = node_out + dot2(both, pair, NT)
    node_out_ref[...] = node_out

    step4(2)

    level_row = lax.broadcasted_iota(jnp.int32, (1, 256), 1)

    def last_body(leaf, acc):
        lhs = jnp.concatenate([coef_buf[far_idx[leaf, s] % 256] for s in range(16)], axis=1)
        leaf_out = dot(lhs, wdup[leaf], NT)
        leaf_out = leaf_out + dot2(node_out_ref[...], ltran[leaf], NN)
        tree = near_acc[leaf] + dot2(leaf_out, basis[leaf], NN)
        local = order[:, pl.ds(pl.multiple_of(leaf * 256, 256), 256)] % 4096
        high = local // 256
        spread = jnp.concatenate(
            [jnp.where(high == h, tree, 0.0).astype(BF16) for h in range(16)], axis=0
        )
        return acc + dot(spread, onehot[leaf], NT)

    acc = lax.fori_loop(0, 16, last_body, jnp.zeros((256, 256), F32))
    for h in range(16):
        out_ref[:, h * 256:(h + 1) * 256] = acc[h * 16:(h + 1) * 16].astype(BF16)
    for copy in sent:
        copy.wait_send()


def on_device(
    vectors, tree_order, near_blocks, near_index, leaf_basis, leaf_coupling, leaf_far,
    leaf_transfer, node_coupling, node_far, node_transfer, slab_coupling, slab_far_partners,
):
    hbm = pl.BlockSpec(memory_space=pltpu.HBM)
    smem = pl.BlockSpec(memory_space=pltpu.SMEM)
    return pl.pallas_call(
        kernel,
        out_shape=jax.ShapeDtypeStruct((16, 4096), BF16),
        in_specs=[hbm] * 9 + [smem] * 4,
        out_specs=pl.BlockSpec(memory_space=pltpu.VMEM),
        scratch_shapes=[
            pltpu.VMEM((16, 4096), BF16),
            pltpu.VMEM((1, 4096), jnp.int32),
            pltpu.VMEM((16, 8, 256, 256), BF16),
            pltpu.VMEM((16, 64, 256), BF16),
            pltpu.VMEM((16, 16, 64, 64), BF16),
            pltpu.VMEM((16, 64, 64), BF16),
            pltpu.VMEM((1, 8, 64, 64), BF16),
            pltpu.VMEM((1, 64, 64), BF16),
            pltpu.VMEM((1, 2, 64, 64), BF16),
            pltpu.VMEM((16, 256, 256), BF16),
            pltpu.VMEM((16, 64, 2048), BF16),
            pltpu.VMEM((256, 16, 128), BF16),
            pltpu.VMEM((256, 16, 128), BF16),
            pltpu.VMEM((256, 16, 128), BF16),
            pltpu.VMEM((4, 4, 16, 128), F32),
            pltpu.VMEM((8, 9, 16, 128), F32),
            pltpu.VMEM((16, 16, 256), F32),
            pltpu.VMEM((16, 64), F32),
            pltpu.SemaphoreType.DMA((8,)),
            pltpu.SemaphoreType.DMA((4,)),
            pltpu.SemaphoreType.DMA((120,)),
            pltpu.SemaphoreType.DMA((120,)),
            pltpu.SemaphoreType.DMA((13,)),
            pltpu.SemaphoreType.DMA((13,)),
        ],
        compiler_params=pltpu.CompilerParams(
            collective_id=0, has_side_effects=True, vmem_limit_bytes=56 << 20
        ),
    )(
        vectors, tree_order.reshape(1, 4096), near_blocks, leaf_basis, leaf_coupling, leaf_transfer,
        node_coupling, node_transfer, slab_coupling,
        near_index.T, leaf_far, node_far, slab_far_partners,
    )


def solution(mesh):
    whole = ("rows", "cols")
    return jax.shard_map(
        on_device,
        mesh=mesh,
        in_specs=(
            P(None, whole), P(whole), P(whole), P(whole), P(whole), P(whole), P(whole),
            P(whole), P(whole), P(whole), P(whole), P("rows"), P("rows"),
        ),
        out_specs=P(None, whole),
        check_vma=False,
    )
```

time: 234 us -> 53.5 us (0.23)
  blocking collectives: 117 us -> 0 us
  Pallas kernels: 0 us -> 51.7 us
  local copies, waits for them, and re-layouts: 51.3 us -> 1.57 us
  waiting for transfers between devices: 31.9 us -> 0 us
  matrix products: 15.6 us -> 0 us
  between operations: 13.7 us -> 0.01 us
  other arithmetic: 3.76 us -> 0 us
    all_gather x2 -> x0, blocking collectives: 77 us -> none  [the longest x1 64.3 us: on_device(): lax.all_gather(node_coef[None], ('rows', 'cols'), axis=0, tiled=True)]
    pallas_call x0 -> x1, Pallas kernels: none -> 51.7 us  [on_device(): pl.pallas_call(kernel, out_shape=jax.ShapeDtypeStruct((16, 4096), BF16),...]
    psum x1 -> x0, blocking collectives: 39.6 us -> none  [on_device(): slab_total = lax.psum(node_term, 'cols')]
    gather x7 -> x0, local copies, waits for them, and re-layouts: 35.2 us -> none  [the longest x2 19.2 us: on_device(): selected_entries = jnp.take(slab_leaves, near_slot, axis=1)]
    all_gather x2 -> x0, waiting for transfers between devices: 31.9 us -> none  [the longest x1 31.9 us: on_device(): slab_vectors = lax.all_gather(tree_vectors, 'cols', axis=1, tiled=True)]
    dot_general x10 -> x0, matrix products: 15.6 us -> none  [the longest x1 8.05 us: on_device(): jnp.einsum('rlsq,lspq->rlp', selected_entries, near_blocks, preferred_ele...]
    scatter x2 -> x0, local copies, waits for them, and re-layouts: 12.4 us -> none  [on_device(): jnp.zeros((rhs_count, points_on_part), jnp.float32).at[:, local_order]]
    select_n x4 -> x0, other arithmetic: 2.92 us -> none  [the longest x1 2.9 us: on_device(): tree_vectors = jnp.take(vectors, local_order, axis=1)]
  transfers between devices with their start and end apart: 2 -> 0, of which waited for: 1 -> 0; matrix products, arithmetic and copies ran while one was open for 6% -> 0% of each run, Pallas kernels for 0% -> 0%
where the time goes in v1:
time: 53.5 us; the launch traced here: 53.3 us
  Pallas kernels  51.7 us (97%)
  local copies, waits for them, and re-layouts  1.57 us (3%)
    pallas_call x1, Pallas kernels, on_device(): pl.pallas_call(kernel, out_shape=jax.ShapeDtypeStruct((16, 4096), BF16),...  51.7 us
    unnamed x1, local copies, waits for them, and re-layouts  1.57 us

profile of v1, /device:TPU:0, one launch (start us, length us, event | category | flops | bytes accessed | tf_op | source)
XLA Modules:
  0.0 53.3 jit_solution(16454536889712759094)
XLA Ops:
  0.0 51.7 %shard_map.127 = bf16[16,4096]{1,0:T(8,128)(2,1)} custom-call(bf16[16,4096]{1,0:T(8,128)(2,1)} %vec_hbm.1, s32[1,4096]{1,0:T(1,128)} %bitcast.2, bf16[16,8,256,256]{3,2,1,0:T(8,128)(2,1)} %near_hbm.1, bf16[16,64,256]{2,1,0:T(8,128)(2,1)} %basis_hbm.1, bf16[16,16,64,64]{3,2,1,0:T(8,128)(2,1)} %coup_hbm.1, bf16[16,64,64]{2,1,0:T(8,128)(2,1)} %ltran_hbm.1, ...), custom_call_target="tpu_custom_call" | custom-call | tf_op jit(solution)/shard_map/pallas_call | solution.py:333
  51.7 1.6 %copy.15 = bf16[16,4096]{1,0:T(8,128)(2,1)} copy(bf16[16,4096]{1,0:T(8,128)(2,1)} %shard_map.127) | data formatting | bytes 262144

commit v2 on v1

v2 whole, which is shorter than its diff:
```python
import jax
import jax.numpy as jnp
from jax import lax
from jax.experimental import pallas as pl
from jax.experimental.pallas import tpu as pltpu
from jax.sharding import PartitionSpec as P

MESH = pl.DeviceIdType.MESH
F32 = jnp.float32
BF16 = jnp.bfloat16

NT = (((1,), (1,)), ((), ()))
NN = (((1,), (0,)), ((), ()))

PLAN = (
    "n0", "x8", "x9", "n1", "c8", "c9", "t0", "x1", "n2", "c1", "t1", "x2", "c2", "t2", "x3",
    "c3", "t3", "x4", "c4", "t4", "x5", "c5", "t5", "x6", "c6", "t6", "t7", "n3", "d0", "d1",
    "d2", "d3", "o", "x7", "N0", "N1", "N2", "N3", "c7", "F", "n4", "L",
)


def dot(a, b, dims):
    return lax.dot_general(a, b, dims, preferred_element_type=F32)


def split2(v):
    high = v.astype(BF16)
    low = (v - high.astype(F32)).astype(BF16)
    return high, low


def dot2(v, b, dims):
    high, low = split2(v)
    rows = v.shape[0]
    both = dot(jnp.concatenate([high, low], axis=0), b, dims)
    return both[:rows] + both[rows:]


def shifted(col, dim, by):
    x, y = col % 4, col // 4
    if dim == 0:
        return y * 4 + (x + by) % 4
    return ((y + by) % 4) * 4 + x


def kernel(
    vec_hbm, ord_hbm, near_hbm, basis_hbm, coup_hbm, ltran_hbm, ncoup_hbm, ntran_hbm, scoup_hbm,
    near_idx, far_idx, node_idx, slab_idx,
    out_ref,
    vec, order, near, basis, coup, ltran, ncoup, ntran, scoup,
    onehot, coup_t, x_buf, coef_buf, node_buf, row_buf, near_acc, leaf_acc, spread,
    in_sem, near_sem, send_sem, recv_sem, nsend, nrecv,
):
    col = lax.axis_index("cols")
    row = lax.axis_index("rows")
    my_x, my_y = col % 4, col // 4

    barrier = pltpu.get_barrier_semaphore()
    partners = [{"cols": shifted(col, dim, by)} for dim in (0, 1) for by in (1, 2, 3)]
    other_core = row + 1 - 2 * (row % 2)
    partners += [{"rows": (row + 2 * by) % 8} for by in (1, 2, 3)] + [{"rows": other_core}]
    for p in partners:
        pl.semaphore_signal(barrier, inc=1, device_id=p, device_id_type=MESH)

    def fetch(src, dst, sem):
        copy = pltpu.make_async_copy(src, dst, sem)
        copy.start()
        return copy

    c_vec = fetch(vec_hbm, vec, in_sem.at[0])
    c_ord = fetch(ord_hbm, order, in_sem.at[1])
    c_basis = fetch(basis_hbm, basis, in_sem.at[2])
    c_ltran = fetch(ltran_hbm, ltran, in_sem.at[3])
    c_ntran = fetch(ntran_hbm, ntran, in_sem.at[4])
    c_near = [
        fetch(near_hbm.at[pl.ds(2 * q, 2)], near.at[pl.ds(2 * q, 2)], near_sem.at[q])
        for q in range(8)
    ]
    c_coup = fetch(coup_hbm, coup, in_sem.at[7])
    c_ncoup = fetch(ncoup_hbm, ncoup, in_sem.at[5])
    c_scoup = fetch(scoup_hbm, scoup, in_sem.at[6])

    sent = []
    buffers = (x_buf, coef_buf)

    def chunk_copy(stage, chunk, first, count, to, k):
        span = buffers[stage].at[pl.ds(chunk * 16 + first, count)]
        return pltpu.make_async_remote_copy(
            span, span, send_sem.at[stage * 40 + k], recv_sem.at[stage * 40 + k],
            device_id={"cols": to}, device_id_type=MESH,
        )

    def send(stage, chunk, first, count, to, k):
        copy = chunk_copy(stage, chunk, first, count, to, k)
        copy.start()
        sent.append(copy)

    def arrived(stage, chunk, first, count, k):
        chunk_copy(stage, chunk, first, count, shifted(col, 0, 1), k).wait_recv()

    def at(half, a, b):
        return shifted(shifted(col, half, a), 1 - half, b)

    def key(half, phase, a, t):
        return half * 20 + (0 if phase == 0 else 4 + 4 * a) + t

    def dim_of(half, phase):
        return half if phase == 0 else 1 - half

    def put(stage, half, phase, a):
        d = dim_of(half, phase)
        chunk = at(half, a, 0) if phase else col
        send(stage, chunk, half * 8, 8, shifted(col, d, 1), key(half, phase, a, 0))
        send(stage, chunk, half * 8, 8, shifted(col, d, 3), key(half, phase, a, 1))

    def source(half, phase, a, by):
        return at(half, a, by) if phase else at(half, by, 0)

    def forward(stage, half, phase, a):
        d = dim_of(half, phase)
        chunk = source(half, phase, a, 3)
        arrived(stage, chunk, half * 8, 8, key(half, phase, a, 0))
        send(stage, chunk, half * 8, 4, shifted(col, d, 1), key(half, phase, a, 2))
        chunk = source(half, phase, a, 1)
        arrived(stage, chunk, half * 8, 8, key(half, phase, a, 1))
        send(stage, chunk, half * 8 + 4, 4, shifted(col, d, 3), key(half, phase, a, 3))

    def finish(stage, half, phase, a):
        chunk = source(half, phase, a, 2)
        arrived(stage, chunk, half * 8, 4, key(half, phase, a, 2))
        arrived(stage, chunk, half * 8 + 4, 4, key(half, phase, a, 3))

    def step(stage, number):
        for half in (0, 1):
            if number == 1:
                forward(stage, half, 0, 0)
            if number == 2:
                finish(stage, half, 0, 0)
            if number in (3, 4, 5, 6):
                forward(stage, half, 1, (0, 1, 3, 2)[number - 3])
        for half in (0, 1):
            if number in (0, 8):
                put(stage, half, 0, 0)
            if number == 1:
                put(stage, half, 1, 1)
            if number == 2:
                put(stage, half, 1, 2)
        for half in (0, 1):
            if number in (0, 9):
                put(stage, half, 1, 0)
            if number == 1:
                put(stage, half, 1, 3)
        if number == 7:
            for a in (0, 1, 3, 2):
                for half in (0, 1):
                    finish(stage, half, 1, a)

    c_vec.wait()
    c_ord.wait()
    lhs = jnp.concatenate([vec[:, h * 256:(h + 1) * 256] for h in range(16)], axis=0)
    level = lax.broadcasted_iota(jnp.int32, (256, 256), 0)
    own = col * 16

    def permute(leaf):
        local = order[:, leaf * 256:(leaf + 1) * 256] % 4096
        low = jnp.broadcast_to(local % 256, (256, 256))
        hot = jnp.where(low == level, 1.0, 0.0).astype(BF16)
        onehot[pl.ds(leaf * 256, 256)] = hot
        part = dot(lhs, hot, NN)
        high = local // 256
        x = jnp.zeros((16, 256), F32)
        for h in range(16):
            x = x + jnp.where(high == h, part[h * 16:(h + 1) * 16], 0.0)
        x_buf[own + leaf] = x.astype(BF16)

    for leaf in range(16):
        permute(leaf)

    c_basis.wait()
    c_ltran.wait()
    c_ntran.wait()
    coefs = []
    for leaf in range(16):
        coef = dot(x_buf[own + leaf], basis[leaf], NT)
        high, low = split2(coef)
        coef_buf[own + leaf] = jnp.concatenate([high, low], axis=1)
        coefs.append(coef)
    node_coef = jnp.zeros((16, 64), F32)
    for leaf in range(16):
        node_coef = node_coef + dot2(coefs[leaf], ltran[leaf], NT)
    node_term = dot2(node_coef, ntran[0], NT)
    pl.semaphore_wait(barrier, len(partners))

    def node_copy(src, k, to):
        return pltpu.make_async_remote_copy(
            src, src, nsend.at[k], nrecv.at[k], device_id=to, device_id_type=MESH
        )

    def node_send(src, k, to):
        copy = node_copy(src, k, to)
        copy.start()
        sent.append(copy)

    def node0():
        node_buf[my_y, my_x] = jnp.concatenate([node_coef, node_term], axis=1)
        for by in (1, 3, 2):
            node_send(node_buf.at[my_y, my_x], by - 1, {"cols": shifted(col, 0, by)})

    def node1():
        for by in (1, 3, 2):
            node_copy(node_buf.at[my_y, (my_x + 4 - by) % 4], by - 1, partners[0]).wait_recv()
        for by in (1, 3, 2):
            node_send(node_buf.at[my_y], 2 + by, {"cols": shifted(col, 1, by)})

    def node2():
        for by in (1, 3, 2):
            node_copy(node_buf.at[(my_y + 4 - by) % 4], 2 + by, partners[0]).wait_recv()
        slab_coef = jnp.zeros((16, 64), F32)
        for m in range(8):
            left, right = node_buf[m // 2, m % 2 * 2], node_buf[m // 2, m % 2 * 2 + 1]
            row_buf[row, m] = jnp.concatenate([left[:, :64], right[:, :64]], axis=1)
            slab_coef = slab_coef + (left[:, 64:] + right[:, 64:])
        row_buf[row, 8] = jnp.concatenate([slab_coef, slab_coef], axis=1)
        for n, by in enumerate((1, 3, 2)):
            node_send(row_buf.at[row], 6 + n, {"rows": (row + 2 * by) % 8})
        node_send(row_buf.at[row], 9, {"rows": other_core})

    def node3():
        for n, by in enumerate((1, 3, 2)):
            source_row = (row + 8 - 2 * by) % 8
            node_copy(row_buf.at[source_row], 6 + n, partners[0]).wait_recv()
            node_send(row_buf.at[source_row], 10 + n, {"rows": other_core})

    def node4():
        node_copy(row_buf.at[other_core], 9, partners[0]).wait_recv()
        for n, by in enumerate((1, 3, 2)):
            source_row = (other_core + 8 - 2 * by) % 8
            node_copy(row_buf.at[source_row], 10 + n, partners[0]).wait_recv()
        c_ncoup.wait()
        c_scoup.wait()
        slab_out = jnp.zeros((16, 64), F32)
        for s in range(2):
            slab_out = slab_out + dot2(row_buf[slab_idx[0, s], 8][:, :64], scoup[0, s], NT)
        node_out = dot2(slab_out, ntran[0], NN)
        lane = lax.broadcasted_iota(jnp.int32, (16, 128), 1)
        for s in range(8):
            d = node_idx[0, s]
            both = row_buf[d // 16, d % 16 // 2]
            both = jnp.where(lane // 64 == d % 2, both, 0.0)
            pair = jnp.concatenate([ncoup[0, s], ncoup[0, s]], axis=1)
            node_out = node_out + dot2(both, pair, NT)
        for leaf in range(16):
            leaf_acc[leaf] = leaf_acc[leaf] + dot2(node_out, ltran[leaf], NN)

    def loop(first, count, body):
        def wrapped(k, carry):
            body(k)
            return carry

        lax.fori_loop(first, first + count, wrapped, 0)

    def turn_near(q):
        c_near[q].wait()

        def body(leaf):
            for s in range(8):
                near[leaf, s] = near[leaf, s].T

        loop(2 * q, 2, body)

    def turn_coup(q):
        if q == 0:
            c_coup.wait()

        def body(leaf):
            for s in range(16):
                m = coup[leaf, s].T
                coup_t[leaf, s * 128:s * 128 + 64] = m
                coup_t[leaf, s * 128 + 64:s * 128 + 128] = m

        loop(4 * q, 4, body)

    def turn_onehot():
        def body(leaf):
            span = pl.ds(pl.multiple_of(leaf * 256, 256), 256)
            onehot[span] = onehot[span].T

        loop(0, 16, body)

    def near_some(q):
        def body(k):
            for u in range(4):
                leaf = 4 * k + u
                x = jnp.concatenate([x_buf[near_idx[s, leaf] % 256] for s in range(8)], axis=1)
                near_acc[leaf] = dot(x, near[leaf].reshape(2048, 256), NN)

        loop(q, 1, body)

    def far_all():
        def body(k):
            for u in range(4):
                leaf = 4 * k + u
                c = jnp.concatenate([coef_buf[far_idx[leaf, s] % 256] for s in range(16)], axis=1)
                leaf_acc[leaf] = dot(c, coup_t[leaf], NN)

        loop(0, 4, body)

    def last():
        for leaf in range(16):
            span = slice(leaf * 256, leaf * 256 + 256)
            tree = near_acc[leaf] + dot2(leaf_acc[leaf], basis[leaf], NN)
            high = order[:, span] % 4096 // 256
            spread[:, span] = jnp.concatenate(
                [jnp.where(high == h, tree, 0.0).astype(BF16) for h in range(16)], axis=0
            )
        total = dot(spread[...], onehot[...], NN)
        for h in range(16):
            out_ref[:, h * 256:(h + 1) * 256] = total[h * 16:(h + 1) * 16].astype(BF16)

    node_steps = (node0, node1, node2, node3, node4)
    for token in PLAN:
        kind, number = token[0], int(token[1:] or 0)
        if kind == "x":
            step(0, number)
        elif kind == "c":
            step(1, number)
        elif kind == "n":
            node_steps[number]()
        elif kind == "t":
            turn_near(number)
        elif kind == "d":
            turn_coup(number)
        elif kind == "o":
            turn_onehot()
        elif kind == "N":
            near_some(number)
        elif kind == "F":
            far_all()
        elif kind == "L":
            last()
    for copy in sent:
        copy.wait_send()


def on_device(
    vectors, tree_order, near_blocks, near_index, leaf_basis, leaf_coupling, leaf_far,
    leaf_transfer, node_coupling, node_far, node_transfer, slab_coupling, slab_far_partners,
):
    hbm = pl.BlockSpec(memory_space=pltpu.HBM)
    smem = pl.BlockSpec(memory_space=pltpu.SMEM)
    return pl.pallas_call(
        kernel,
        out_shape=jax.ShapeDtypeStruct((16, 4096), BF16),
        in_specs=[hbm] * 9 + [smem] * 4,
        out_specs=pl.BlockSpec(memory_space=pltpu.VMEM),
        scratch_shapes=[
            pltpu.VMEM((16, 4096), BF16),
            pltpu.VMEM((1, 4096), jnp.int32),
            pltpu.VMEM((16, 8, 256, 256), BF16),
            pltpu.VMEM((16, 64, 256), BF16),
            pltpu.VMEM((16, 16, 64, 64), BF16),
            pltpu.VMEM((16, 64, 64), BF16),
            pltpu.VMEM((1, 8, 64, 64), BF16),
            pltpu.VMEM((1, 64, 64), BF16),
            pltpu.VMEM((1, 2, 64, 64), BF16),
            pltpu.VMEM((4096, 256), BF16),
            pltpu.VMEM((16, 2048, 64), BF16),
            pltpu.VMEM((256, 16, 256), BF16),
            pltpu.VMEM((256, 16, 128), BF16),
            pltpu.VMEM((4, 4, 16, 128), F32),
            pltpu.VMEM((8, 9, 16, 128), F32),
            pltpu.VMEM((16, 16, 256), F32),
            pltpu.VMEM((16, 16, 64), F32),
            pltpu.VMEM((256, 4096), BF16),
            pltpu.SemaphoreType.DMA((8,)),
            pltpu.SemaphoreType.DMA((8,)),
            pltpu.SemaphoreType.DMA((80,)),
            pltpu.SemaphoreType.DMA((80,)),
            pltpu.SemaphoreType.DMA((13,)),
            pltpu.SemaphoreType.DMA((13,)),
        ],
        compiler_params=pltpu.CompilerParams(
            collective_id=0, has_side_effects=True, vmem_limit_bytes=56 << 20
        ),
    )(
        vectors, tree_order.reshape(1, 4096), near_blocks, leaf_basis, leaf_coupling, leaf_transfer,
        node_coupling, node_transfer, slab_coupling,
        near_index.T, leaf_far, node_far, slab_far_partners,
    )


def solution(mesh):
    whole = ("rows", "cols")
    return jax.shard_map(
        on_device,
        mesh=mesh,
        in_specs=(
            P(None, whole), P(whole), P(whole), P(whole), P(whole), P(whole), P(whole),
            P(whole), P(whole), P(whole), P(whole), P("rows"), P("rows"),
        ),
        out_specs=P(None, whole),
        check_vma=False,
    )
```

time: 53.5 us -> 39.4 us (0.74)
  Pallas kernels: 51.7 us -> 37.6 us
    pallas_call x1, Pallas kernels: 51.7 us -> 37.6 us  [on_device(): pl.pallas_call(kernel, out_shape=jax.ShapeDtypeStruct((16, 4096), BF16),...]
where the time goes in v2:
time: 39.4 us; the launch traced here: 39.2 us
  Pallas kernels  37.6 us (95%)
  local copies, waits for them, and re-layouts  1.57 us (4%)
    pallas_call x1, Pallas kernels, on_device(): pl.pallas_call(kernel, out_shape=jax.ShapeDtypeStruct((16, 4096), BF16),...  37.6 us
    unnamed x1, local copies, waits for them, and re-layouts  1.57 us

profile of v2, /device:TPU:0, one launch (start us, length us, event | category | flops | bytes accessed | tf_op | source)
XLA Modules:
  0.0 39.2 jit_solution(7542048016066711009)
XLA Ops:
  0.0 37.6 %shard_map.127 = bf16[16,4096]{1,0:T(8,128)(2,1)} custom-call(bf16[16,4096]{1,0:T(8,128)(2,1)} %vec_hbm.1, s32[1,4096]{1,0:T(1,128)} %bitcast.2, bf16[16,8,256,256]{3,2,1,0:T(8,128)(2,1)} %near_hbm.1, bf16[16,64,256]{2,1,0:T(8,128)(2,1)} %basis_hbm.1, bf16[16,16,64,64]{3,2,1,0:T(8,128)(2,1)} %coup_hbm.1, bf16[16,64,64]{2,1,0:T(8,128)(2,1)} %ltran_hbm.1, ...), custom_call_target="tpu_custom_call" | custom-call | tf_op jit(solution)/shard_map/pallas_call | solution.py:351
  37.6 1.6 %copy.15 = bf16[16,4096]{1,0:T(8,128)(2,1)} copy(bf16[16,4096]{1,0:T(8,128)(2,1)} %shard_map.127) | data formatting | bytes 262144

commit v3 on v2

--- a/solution.py
+++ b/solution.py
@@ -13,9 +13,9 @@
 NN = (((1,), (0,)), ((), ()))
 
 PLAN = (
-    "n0", "x8", "x9", "n1", "c8", "c9", "t0", "x1", "n2", "c1", "t1", "x2", "c2", "t2", "x3",
-    "c3", "t3", "x4", "c4", "t4", "x5", "c5", "t5", "x6", "c6", "t6", "t7", "n3", "d0", "d1",
-    "d2", "d3", "o", "x7", "N0", "N1", "N2", "N3", "c7", "F", "n4", "L",
+    "n0", "c8", "x8", "c9", "x9", "n1", "t0", "c1", "x1", "n2", "t1", "c2", "x2", "t2", "d0",
+    "c3", "x3", "t3", "d1", "c4", "x4", "t4", "d2", "c5", "x5", "t5", "d3", "c6", "x6", "n3",
+    "t6", "t7", "o", "c7", "F", "n4", "P", "x7", "N0", "N1", "N2", "N3", "L",
 )
 
 
@@ -45,8 +45,9 @@
 
 def kernel(
     vec_hbm, ord_hbm, near_hbm, basis_hbm, coup_hbm, ltran_hbm, ncoup_hbm, ntran_hbm, scoup_hbm,
+    near_idx_hbm, far_idx_hbm, node_idx_hbm, slab_idx_hbm,
+    out_ref,
     near_idx, far_idx, node_idx, slab_idx,
-    out_ref,
     vec, order, near, basis, coup, ltran, ncoup, ntran, scoup,
     onehot, coup_t, x_buf, coef_buf, node_buf, row_buf, near_acc, leaf_acc, spread,
     in_sem, near_sem, send_sem, recv_sem, nsend, nrecv,
@@ -69,6 +70,12 @@
 
     c_vec = fetch(vec_hbm, vec, in_sem.at[0])
     c_ord = fetch(ord_hbm, order, in_sem.at[1])
+    c_lists = [
+        fetch(near_idx_hbm, near_idx, in_sem.at[8]),
+        fetch(far_idx_hbm, far_idx, in_sem.at[9]),
+        fetch(node_idx_hbm, node_idx, in_sem.at[10]),
+        fetch(slab_idx_hbm, slab_idx, in_sem.at[11]),
+    ]
     c_basis = fetch(basis_hbm, basis, in_sem.at[2])
     c_ltran = fetch(ltran_hbm, ltran, in_sem.at[3])
     c_ntran = fetch(ntran_hbm, ntran, in_sem.at[4])
@@ -177,6 +184,8 @@
         permute(leaf)
 
     c_basis.wait()
+    for copy in c_lists:
+        copy.wait()
     c_ltran.wait()
     c_ntran.wait()
     coefs = []
@@ -292,7 +301,7 @@
             for u in range(4):
                 leaf = 4 * k + u
                 x = jnp.concatenate([x_buf[near_idx[s, leaf] % 256] for s in range(8)], axis=1)
-                near_acc[leaf] = dot(x, near[leaf].reshape(2048, 256), NN)
+                near_acc[leaf] = near_acc[leaf] + dot(x, near[leaf].reshape(2048, 256), NN)
 
         loop(q, 1, body)
 
@@ -305,10 +314,14 @@
 
         loop(0, 4, body)
 
+    def far_points():
+        for leaf in range(16):
+            near_acc[leaf] = dot2(leaf_acc[leaf], basis[leaf], NN)
+
     def last():
         for leaf in range(16):
             span = slice(leaf * 256, leaf * 256 + 256)
-            tree = near_acc[leaf] + dot2(leaf_acc[leaf], basis[leaf], NN)
+            tree = near_acc[leaf]
             high = order[:, span] % 4096 // 256
             spread[:, span] = jnp.concatenate(
                 [jnp.where(high == h, tree, 0.0).astype(BF16) for h in range(16)], axis=0
@@ -336,6 +349,8 @@
             near_some(number)
         elif kind == "F":
             far_all()
+        elif kind == "P":
+            far_points()
         elif kind == "L":
             last()
     for copy in sent:
@@ -347,13 +362,16 @@
     leaf_transfer, node_coupling, node_far, node_transfer, slab_coupling, slab_far_partners,
 ):
     hbm = pl.BlockSpec(memory_space=pltpu.HBM)
-    smem = pl.BlockSpec(memory_space=pltpu.SMEM)
     return pl.pallas_call(
         kernel,
-        out_shape=jax.ShapeDtypeStruct((16, 4096), BF16),
-        in_specs=[hbm] * 9 + [smem] * 4,
+        out_shape=pltpu.VMEM((16, 4096), BF16),
+        in_specs=[hbm] * 13,
         out_specs=pl.BlockSpec(memory_space=pltpu.VMEM),
         scratch_shapes=[
+            pltpu.SMEM((8, 16), jnp.int32),
+            pltpu.SMEM((16, 16), jnp.int32),
+            pltpu.SMEM((1, 8), jnp.int32),
+            pltpu.SMEM((1, 2), jnp.int32),
             pltpu.VMEM((16, 4096), BF16),
             pltpu.VMEM((1, 4096), jnp.int32),
             pltpu.VMEM((16, 8, 256, 256), BF16),
@@ -372,7 +390,7 @@
             pltpu.VMEM((16, 16, 256), F32),
             pltpu.VMEM((16, 16, 64), F32),
             pltpu.VMEM((256, 4096), BF16),
-            pltpu.SemaphoreType.DMA((8,)),
+            pltpu.SemaphoreType.DMA((12,)),
             pltpu.SemaphoreType.DMA((8,)),
             pltpu.SemaphoreType.DMA((80,)),
             pltpu.SemaphoreType.DMA((80,)),

time: 39.4 us -> 34.1 us (0.87)
  Pallas kernels: 37.6 us -> 33.3 us
  local copies, waits for them, and re-layouts: 1.57 us -> 0.66 us
    pallas_call x1, Pallas kernels: 37.6 us -> 33.3 us  [on_device(): pl.pallas_call(kernel, out_shape=pltpu.VMEM((16, 4096), BF16), in_specs=[...]
    unnamed x1, local copies, waits for them, and re-layouts: 1.57 us -> 0.66 us
where the time goes in v3:
time: 34.1 us; the launch traced here: 34 us
  Pallas kernels  33.3 us (98%)
  local copies, waits for them, and re-layouts  0.66 us (2%)
    pallas_call x1, Pallas kernels, on_device(): pl.pallas_call(kernel, out_shape=pltpu.VMEM((16, 4096), BF16), in_specs=[...  33.3 us

profile of v3, /device:TPU:0, one launch (start us, length us, event | category | flops | bytes accessed | tf_op | source)
XLA Modules:
  0.0 34.0 jit_solution(7963889973618905978)
XLA Ops:
  0.0 33.3 %shard_map.127 = bf16[16,4096]{1,0:T(8,128)(2,1)S(1)} custom-call(bf16[16,4096]{1,0:T(8,128)(2,1)} %vec_hbm.1, s32[1,4096]{1,0:T(1,128)} %bitcast.2, bf16[16,8,256,256]{3,2,1,0:T(8,128)(2,1)} %near_hbm.1, bf16[16,64,256]{2,1,0:T(8,128)(2,1)} %basis_hbm.1, bf16[16,16,64,64]{3,2,1,0:T(8,128)(2,1)} %coup_hbm.1, bf16[16,64,64]{2,1,0:T(8,128)(2,1)} %ltran_hbm.1, ...), custom_call_target="tpu_custom_call" | custom-call | tf_op jit(solution)/shard_map/pallas_call | solution.py:365
  33.3 0.7 %copy.15 = bf16[16,4096]{1,0:T(8,128)(2,1)} copy(bf16[16,4096]{1,0:T(8,128)(2,1)S(1)} %shard_map.127) | data formatting | bytes 262144

commit v4 on v3

--- a/solution.py
+++ b/solution.py
@@ -13,9 +13,10 @@
 NN = (((1,), (0,)), ((), ()))
 
 PLAN = (
-    "n0", "c8", "x8", "c9", "x9", "n1", "t0", "c1", "x1", "n2", "t1", "c2", "x2", "t2", "d0",
-    "c3", "x3", "t3", "d1", "c4", "x4", "t4", "d2", "c5", "x5", "t5", "d3", "c6", "x6", "n3",
-    "t6", "t7", "o", "c7", "F", "n4", "P", "x7", "N0", "N1", "N2", "N3", "L",
+    "n0", "c8", "x8", "c9", "x9", "n1", "t0", "c1", "t1", "x1", "t2", "n2", "t3", "c2", "t4",
+    "x2", "d0", "c3", "d1", "t5", "x3", "t6", "d2", "c4", "t7", "d3", "x4", "t8", "d4", "c5",
+    "t9", "d5", "x5", "t10", "d6", "c6", "t11", "d7", "x6", "n3", "t12", "t13", "t14", "t15",
+    "o", "c7", "F", "n4", "P", "x7", "N0", "N1", "N2", "N3", "L",
 )
 
 
@@ -269,13 +270,10 @@
         lax.fori_loop(first, first + count, wrapped, 0)
 
     def turn_near(q):
-        c_near[q].wait()
-
-        def body(leaf):
-            for s in range(8):
-                near[leaf, s] = near[leaf, s].T
-
-        loop(2 * q, 2, body)
+        if q % 2 == 0:
+            c_near[q // 2].wait()
+        for s in range(8):
+            near[q, s] = near[q, s].T
 
     def turn_coup(q):
         if q == 0:
@@ -287,7 +285,7 @@
                 coup_t[leaf, s * 128:s * 128 + 64] = m
                 coup_t[leaf, s * 128 + 64:s * 128 + 128] = m
 
-        loop(4 * q, 4, body)
+        loop(2 * q, 2, body)
 
     def turn_onehot():
         def body(leaf):

time: 34.1 us -> 33.1 us (0.971)
  Pallas kernels: 33.3 us -> 32.4 us
    pallas_call x1, Pallas kernels: 33.3 us -> 32.4 us  [on_device(): pl.pallas_call(kernel, out_shape=pltpu.VMEM((16, 4096), BF16), in_specs=[...]
where the time goes in v4:
time: 33.1 us; the launch traced here: 33 us
  Pallas kernels  32.4 us (98%)
  local copies, waits for them, and re-layouts  0.66 us (2%)
    pallas_call x1, Pallas kernels, on_device(): pl.pallas_call(kernel, out_shape=pltpu.VMEM((16, 4096), BF16), in_specs=[...  32.4 us

profile of v4, /device:TPU:0, one launch (start us, length us, event | category | flops | bytes accessed | tf_op | source)
XLA Modules:
  0.0 33.0 jit_solution(6734491907327826739)
XLA Ops:
  0.0 32.4 %shard_map.127 = bf16[16,4096]{1,0:T(8,128)(2,1)S(1)} custom-call(bf16[16,4096]{1,0:T(8,128)(2,1)} %vec_hbm.1, s32[1,4096]{1,0:T(1,128)} %bitcast.2, bf16[16,8,256,256]{3,2,1,0:T(8,128)(2,1)} %near_hbm.1, bf16[16,64,256]{2,1,0:T(8,128)(2,1)} %basis_hbm.1, bf16[16,16,64,64]{3,2,1,0:T(8,128)(2,1)} %coup_hbm.1, bf16[16,64,64]{2,1,0:T(8,128)(2,1)} %ltran_hbm.1, ...), custom_call_target="tpu_custom_call" | custom-call | tf_op jit(solution)/shard_map/pallas_call | solution.py:363
  32.4 0.7 %copy.15 = bf16[16,4096]{1,0:T(8,128)(2,1)} copy(bf16[16,4096]{1,0:T(8,128)(2,1)S(1)} %shard_map.127) | data formatting | bytes 262144

commit v5 on v4

--- a/solution.py
+++ b/solution.py
@@ -61,7 +61,7 @@
     partners = [{"cols": shifted(col, dim, by)} for dim in (0, 1) for by in (1, 2, 3)]
     other_core = row + 1 - 2 * (row % 2)
     partners += [{"rows": (row + 2 * by) % 8} for by in (1, 2, 3)] + [{"rows": other_core}]
-    for p in partners:
+    for p in partners[6:] + partners[:6]:
         pl.semaphore_signal(barrier, inc=1, device_id=p, device_id_type=MESH)
 
     def fetch(src, dst, sem):

time: 33.1 us -> 33.1 us (level)
  no operation moved by 1% of the time
where the time goes in v5:
time: 33.1 us; the launch traced here: 33 us
  Pallas kernels  32.4 us (98%)
  local copies, waits for them, and re-layouts  0.66 us (2%)
    pallas_call x1, Pallas kernels, on_device(): pl.pallas_call(kernel, out_shape=pltpu.VMEM((16, 4096), BF16), in_specs=[...  32.4 us

profile of v5, /device:TPU:0, one launch (start us, length us, event | category | flops | bytes accessed | tf_op | source)
XLA Modules:
  0.0 33.0 jit_solution(15407190563627502896)
XLA Ops:
  0.0 32.4 %shard_map.127 = bf16[16,4096]{1,0:T(8,128)(2,1)S(1)} custom-call(bf16[16,4096]{1,0:T(8,128)(2,1)} %vec_hbm.1, s32[1,4096]{1,0:T(1,128)} %bitcast.2, bf16[16,8,256,256]{3,2,1,0:T(8,128)(2,1)} %near_hbm.1, bf16[16,64,256]{2,1,0:T(8,128)(2,1)} %basis_hbm.1, bf16[16,16,64,64]{3,2,1,0:T(8,128)(2,1)} %coup_hbm.1, bf16[16,64,64]{2,1,0:T(8,128)(2,1)} %ltran_hbm.1, ...), custom_call_target="tpu_custom_call" | custom-call | tf_op jit(solution)/shard_map/pallas_call | solution.py:363
  32.4 0.7 %copy.15 = bf16[16,4096]{1,0:T(8,128)(2,1)} copy(bf16[16,4096]{1,0:T(8,128)(2,1)S(1)} %shard_map.127) | data formatting | bytes 262144
